TPU v7x, 128 devices: a whole 4x4x4 slice. The times are simulated.
128 devices in a mesh: owner: 32 (over x, y, core), rep: 4 (over z).
Axes of the slice: x: 4, y: 4, z: 4, core: 2. Of those that a mesh axis runs over, the one named last changes fastest.
Arguments:
- embeddings: bfloat16 [32768, 1024], P(('owner', 'rep')), may hold values from -16 to 16
- cluster: int32 [32768], P(('owner', 'rep')), may hold values from 0 to 15, as said below
Outputs:
- best: float32 [32768], P(('owner', 'rep'))
Inputs may be any that keep to these rules, and one draw needn't show every extreme that they name: `cluster`: the clusters c with the same c // 4 form a group. Among the rows of one device at most 128 lie in one group; in every draw one group holds exactly 128 rows of every device.
All inputs are finite; a program needn't handle non-finite values.
Results may differ from a plain program's by a relative error of at most 0.00062.
Values may be sent and summed in bfloat16 or wider, within the bound.
A program may use at most 128 MiB of HBM per device.

v0:
```python
import jax
import jax.numpy as jnp
from jax import lax
from jax.sharding import PartitionSpec as P

CL_GRP = 4


def normalize(embeddings):
    values = embeddings.astype(jnp.float32)
    factor = lax.rsqrt(
        jnp.mean(values * values, axis=-1, keepdims=True) + 1e-06
    ) * embeddings.shape[-1] ** (-0.5)
    return (values * factor).astype(jnp.bfloat16)


def masked_scores(left, left_meta, right, right_meta):
    scores = lax.dot_general(
        left, right, (((1,), (1,)), ((), ())), preferred_element_type=jnp.float32
    )
    left_cluster = left_meta[:, 0][:, None]
    same = (left_cluster == right_meta[:, 0][None, :]) & (left_cluster >= 0)
    same = same & (left_meta[:, 1][:, None] != right_meta[:, 1][None, :])
    return jnp.where(same, scores, jnp.float32(-1.0))


def on_device(embeddings, cluster):
    rows = embeddings.shape[0]
    width = embeddings.shape[1]
    groups = lax.axis_size("rep")
    capacity = 2 * rows // groups
    slots = groups * capacity
    unit = normalize(embeddings)
    target = cluster // CL_GRP
    onehot = (target[:, None] == jnp.arange(groups, dtype=jnp.int32)[None, :]).astype(jnp.int32)
    before = jnp.cumsum(onehot, axis=0) - onehot
    place = target * capacity + jnp.sum(before * onehot, axis=1)
    device = lax.axis_index("owner") * groups + lax.axis_index("rep")
    row_ids = device * rows + jnp.arange(rows, dtype=jnp.int32)
    outgoing = jnp.zeros((slots, width), jnp.bfloat16).at[place].set(unit)
    labels = (
        jnp.full((slots, 2), -1, jnp.int32).at[place].set(jnp.stack([cluster, row_ids], axis=1))
    )
    arrived, arrived_meta = (
        lax.all_to_all(
            outgoing.reshape(groups, capacity, width),
            "rep",
            split_axis=0,
            concat_axis=0,
            tiled=True,
        ),
        lax.all_to_all(
            labels.reshape(groups, capacity, 2), "rep", split_axis=0, concat_axis=0, tiled=True
        ),
    )
    members = arrived.reshape(slots, width)
    member_meta = arrived_meta.reshape(slots, 2)
    start_best = jnp.full((slots,), -1.0, jnp.float32)
    tile = masked_scores(
        members,
        member_meta,
        lax.all_gather(members, "owner", axis=0, tiled=True),
        lax.all_gather(member_meta, "owner", axis=0, tiled=True),
    )
    best = jnp.maximum(start_best, jnp.max(tile, axis=1))
    homeward = lax.all_to_all(
        best.reshape(groups, capacity), "rep", split_axis=0, concat_axis=0, tiled=True
    )
    return homeward.reshape(slots)[place]


def solution(mesh):
    return jax.shard_map(
        on_device,
        mesh=mesh,
        in_specs=(P(("owner", "rep"), None), P(("owner", "rep"))),
        out_specs=P(("owner", "rep")),
        check_vma=False,
    )
```

profile of v0, /device:TPU:1, one launch (start us, length us, event | category | flops | bytes accessed | tf_op | source)
XLA Modules:
  0.0 194.3 jit_solution(6937393998002297517)
XLA Ops:
  6.5 0.0 all-gather.2.cloned.1.call-start
  6.5 0.7 fusion.15
  7.2 0.7 and_select_fusion
  7.9 1.2 reduce-window.6
  9.1 0.1 slice.26
  9.2 0.1 copy.11
  9.4 0.1 copy.12
  9.5 0.1 add_bitcast_fusion
  9.6 0.7 compare_select_fusion
  10.3 1.2 fusion
  11.5 2.5 %scatter_custom_fusion.1 = bf16[512,1024]{1,0:T(8,128)(2,1)S(1)} fusion(s32[256]{0:T(256)S(1)} %compare_select_fusion, bf16[256,1024]{1,0:T(8,128)(2,1)} %param.2, f32[256]{0:T(256)S(1)} %rsqrt_multiply_fusion, bf16[]{:T(256)} %constant.49.clone.1), kind=kCustom, calls=%fused_computation.8 | custom fusion | flops 786432 | bytes 1573890 | tf_op jit(solution)/shard_map/scatter | solution.py:40
  14.0 19.9 %all_to_all.16 = bf16[4,128,1024]{2,1,0:T(8,128)(2,1)} all-to-all(bf16[4,128,1024]{2,1,0:T(8,128)(2,1)S(1)} %bitcast.37), channel_id=1, replica_groups=mesh['owner'=32,'rep'=4] {'rep'}, dimensions={0} | all-to-all | bytes 2097152 | tf_op jit(solution)/shard_map/all_to_all | solution.py:45
  33.9 0.0 all-gather.2.cloned.1.call-update
  34.0 0.7 pad_add_fusion
  34.7 0.1 copy.13
  34.8 1.2 scatter_custom_fusion
  36.0 0.1 copy.14
  36.1 6.5 %all_to_all.17 = s32[4,128,2]{1,2,0:T(2,128)S(1)} all-to-all(s32[4,128,2]{1,2,0:T(2,128)S(1)} %copy.14), channel_id=1, replica_groups=mesh['owner'=32,'rep'=4] {'rep'}, dimensions={0} | all-to-all | bytes 8192 | tf_op jit(solution)/shard_map/all_to_all | solution.py:52
  42.6 27.8 %all_gather.6 = s32[16384,2]{0,1:T(2,128)S(1)} all-gather(s32[512,2]{0,1:T(2,128)S(1)} %bitcast.41), channel_id=1, replica_groups=mesh['owner'=32,'rep'=4] {'owner'}, dimensions={0}, use_global_device_ids=true | all-gather | bytes 135168 | tf_op jit(solution)/shard_map/all_gather | solution.py:63
  70.4 0.1 fusion.11
  70.6 78.5 %all-gather.2.cloned.1.call-done = bf16[16384,1024]{1,0:T(8,128)(2,1)} async-done(((bf16[512,1024]{1,0:T(8,128)(2,1)}), bf16[16384,1024]{1,0:T(8,128)(2,1)}) %all-gather.2.cloned.1.call-update) | async-done | bytes 33554448 | tf_op jit(solution)/shard_map/all_gather | solution.py:62
  149.0 27.1 %select_reduce_fusion = f32[512]{0:T(512)S(1)} fusion(bf16[512,1024]{1,0:T(8,128)(2,1)} %bitcast.36, bf16[16384,1024]{1,0:T(8,128)(2,1)} %all-gather.2.cloned.1.call-done, s32[16384]{0:T(1024)S(1)} %bitcast.40, s32[16384]{0:T(1024)S(1)} %bitcast.39, s32[512]{0:T(512)S(1)} %bitcast.47, s32[512]{0:T(512)S(1)} %bitcast.46, pred[512]{0:T(512)(128)(4,1)S(1)} %compare_reduce_fusion), kind=kOutput, calls=%fused_computation.3 | convolution fusion | flops 17230200832 | bytes 34740736 | tf_op jit(solution)/shard_map/dot_general | solution.py:18
  176.1 0.6 broadcast_maximum_fusion
  176.7 4.1 %all-to-all-start.2 = ((f32[4,1,128]{2,1,0:T(1,128)}), f32[4,1,128]{2,1,0:T(1,128)S(1)}, u32[]{:S(2)}, u32[]{:S(2)}) async-start(f32[4,1,128]{2,1,0:T(1,128)} %bitcast.12), calls=%async_computation.2 | async-start | bytes 4096 | tf_op jit(solution)/shard_map/all_to_all | solution.py:66
  180.9 4.1 %all-to-all-done.2 = f32[4,1,128]{2,1,0:T(1,128)S(1)} async-done(((f32[4,1,128]{2,1,0:T(1,128)}), f32[4,1,128]{2,1,0:T(1,128)S(1)}, u32[]{:S(2)}, u32[]{:S(2)}) %all-to-all-start.2) | async-done | bytes 2080 | tf_op jit(solution)/shard_map/all_to_all | solution.py:66
  185.0 2.5 %gather_fusion = f32[256]{0:T(256)} fusion(f32[512]{0:T(512)S(1)} %bitcast.34, s32[1024]{0:T(1024)S(1)} %pad_clamp_fusion), kind=kCustom, calls=%fused_computation | custom fusion | bytes 3072 | tf_op jit(solution)/shard_map/gather | solution.py:69
  (9 shorter events, 0.1 us)
Async XLA Ops:
  6.5 142.5 %all-gather.2.cloned.1.call-start = ((), (), s32[]{:S(2)}) async-start(), calls=%async_computation.3 | async-start | bytes 34603008 | tf_op jit(solution)/shard_map/all_gather | solution.py:62
  176.7 8.2 %all-to-all-start.2 = ((f32[4,1,128]{2,1,0:T(1,128)}), f32[4,1,128]{2,1,0:T(1,128)S(1)}, u32[]{:S(2)}, u32[]{:S(2)}) async-start(f32[4,1,128]{2,1,0:T(1,128)} %bitcast.12), calls=%async_computation.2 | async-start | bytes 4096 | tf_op jit(solution)/shard_map/all_to_all | solution.py:66
Sparse Core Ops, SparseCore 0:
  34.1 114.9 all-gather.1
where the time goes:
time: 195 us; the launch traced here: 194 us
  waiting for transfers between devices  82.6 us (42%)
  blocking collectives  54.2 us (28%)
  matrix products  27.1 us (14%)
  between operations  13.5 us (7%)
  other arithmetic  8.47 us (4%)
  local copies, waits for them, and re-layouts  4.36 us (2%)
  starting transfers between devices  4.14 us (2%)
    all_gather x1, waiting for transfers between devices, on_device(): lax.all_gather(members, 'owner', axis=0, tiled=True)  78.5 us
    all_gather x1, blocking collectives, on_device(): lax.all_gather(member_meta, 'owner', axis=0, tiled=True)  27.8 us
    dot_general x1, matrix products, masked_scores(): lax.dot_general(left, right, (((1,), (1,)), ((), ())), preferred_element_...  27.1 us
    all_to_all x1, blocking collectives, on_device(): lax.all_to_all(outgoing.reshape(groups, capacity, width), 'rep', split_ax...  19.9 us
    all_to_all x1, blocking collectives, on_device(): lax.all_to_all(labels.reshape(groups, capacity, 2), 'rep', split_axis=0,...  6.48 us
    all_to_all x1, starting transfers between devices, on_device(): lax.all_to_all(best.reshape(groups, capacity), 'rep', split_axis=0, conca...  4.13 us
    all_to_all x1, waiting for transfers between devices, on_device(): lax.all_to_all(best.reshape(groups, capacity), 'rep', split_axis=0, conca...  4.1 us
  transfers between devices with their start and end apart: 2, of which 2 were waited for; matrix products, arithmetic and copies ran while one was open for 1% of the time, Pallas kernels for 0%

commit v1 on v0

v1 whole, which is shorter than its diff:
```python
import jax
import jax.numpy as jnp
from jax import lax
from jax.experimental import pallas as pl
from jax.experimental.pallas import tpu as pltpu
from jax.sharding import PartitionSpec as P

MESH = pl.DeviceIdType.MESH
SIDE = 4
STEPS = ((1, 0, 0), (-1, 0, 0), (0, 1, 0), (0, -1, 0), (0, 0, 1), (0, 0, -1))
CHUNKS = 4
SPOTS = (
    (0, 0, 0),
    (0, 1, 0),
    (0, 3, 0),
    (1, 0, 0),
    (3, 0, 0),
    (1, 0, 1),
    (1, 3, 0),
    (0, 1, 3),
    (1, 1, 1),
    (0, 1, 2),
    (3, 1, 3),
    (2, 3, 0),
)
LEFT = (0, 1, 2, 3, 4, 5, 6, 7, 8, 9)
PARENT = (
    (
        (-1, 0, 0, 0, 0, 3, 2, 1, 5, 7, 7, 6),
        (-1, 0, 0, 0, 0, 3, 3, 1, 5, 7, 7, 6),
        (-1, 0, 0, 0, 0, 3, 2, 1, 5, 7, 7, 6),
        (-1, 0, 0, 0, 0, 3, 3, 1, 5, 7, 7, 6),
    ),
    (
        (-1, 0, 0, 0, 0, 3, 2, 1, 5, 7, 7, 6),
        (-1, 0, 0, 0, 0, 3, 3, 1, 5, 7, 7, 6),
        (-1, 0, 0, 0, 0, 3, 3, 1, 5, 7, 7, 6),
        (-1, 0, 0, 0, 0, 3, 3, 1, 5, 7, 7, 6),
    ),
)
WAY = (
    (
        (-1, 2, 3, 0, 1, 4, 0, 5, 2, 5, 1, 0),
        (-1, 2, 3, 0, 1, 4, 3, 5, 2, 5, 1, 0),
        (-1, 2, 3, 0, 1, 4, 0, 5, 2, 5, 1, 0),
        (-1, 2, 3, 0, 1, 4, 3, 5, 2, 5, 1, 0),
    ),
    (
        (-1, 2, 3, 0, 1, 4, 0, 5, 2, 5, 1, 0),
        (-1, 2, 3, 0, 1, 4, 3, 5, 2, 5, 1, 0),
        (-1, 2, 3, 0, 1, 4, 3, 5, 2, 5, 1, 0),
        (-1, 2, 3, 0, 1, 4, 3, 5, 2, 5, 1, 0),
    ),
)
ORDER = (
    (
        (1, 2, 3, 5, 6, 7, 4, 8, 9, 10, 11),
        (1, 3, 5, 6, 7, 2, 4, 8, 9, 10, 11),
        (1, 2, 3, 5, 6, 7, 4, 8, 9, 10, 11),
        (1, 3, 5, 6, 7, 2, 4, 8, 9, 10, 11),
    ),
    (
        (1, 2, 3, 5, 6, 7, 4, 8, 9, 10, 11),
        (1, 3, 5, 6, 7, 2, 4, 8, 9, 10, 11),
        (1, 3, 5, 6, 7, 2, 4, 8, 9, 10, 11),
        (1, 3, 5, 6, 7, 2, 4, 8, 9, 10, 11),
    ),
)
TASKS = (
    (2, 0), (3, 0, 0), (4, 0), (0, 1, 0), (0, 2, 0), (0, 3, 0), (0, 4, 0), (0, 1, 1), (0, 2, 1), (0, 3, 1),
    (0, 4, 1), (0, 5, 0), (0, 7, 0), (0, 1, 2), (0, 2, 2), (0, 3, 2), (0, 4, 2), (0, 5, 1), (0, 7, 1),
    (0, 1, 3), (1, 1), (0, 2, 3), (1, 2), (0, 3, 3), (1, 3), (0, 4, 3), (1, 4), (0, 9, 0), (2, 1), (3, 0, 1),
    (4, 1), (0, 5, 2), (2, 2), (3, 1, 2), (4, 2), (2, 3), (3, 0, 3), (3, 1, 3), (0, 6, 0), (0, 6, 1),
    (0, 8, 0), (0, 10, 0), (3, 2, 3), (4, 3), (0, 5, 3), (1, 5), (0, 7, 2), (2, 4), (3, 3, 4), (4, 4),
    (0, 6, 2), (2, 5), (3, 0, 5), (0, 8, 1), (0, 10, 1), (3, 1, 5), (0, 9, 1), (3, 2, 5), (0, 6, 3), (1, 6),
    (3, 3, 5), (0, 11, 0), (3, 4, 5), (4, 5), (0, 8, 2), (0, 7, 3), (1, 7), (0, 10, 2), (2, 6), (3, 1, 6),
    (0, 11, 1), (3, 4, 6), (3, 5, 6), (4, 6), (2, 7), (3, 0, 7), (3, 2, 7), (0, 8, 3), (1, 8), (3, 4, 7),
    (0, 9, 2), (0, 10, 3), (3, 5, 7), (0, 11, 2), (3, 6, 7), (4, 7), (2, 8), (3, 4, 8), (3, 7, 8), (4, 8),
    (5, 7, 0), (5, 7, 1), (2, 10), (3, 3, 10), (0, 9, 3), (1, 9), (3, 5, 10), (0, 11, 3), (3, 6, 10),
    (3, 8, 10), (4, 10), (5, 3, 0), (5, 3, 1), (5, 10, 0), (2, 9), (3, 0, 9), (3, 1, 9), (3, 2, 9), (3, 4, 9),
    (3, 5, 9), (3, 6, 9), (3, 8, 9), (4, 9), (5, 6, 0), (5, 6, 1), (5, 5, 0), (5, 5, 1), (5, 4, 0), (5, 4, 1),
    (5, 2, 0), (5, 2, 1), (5, 0, 1), (2, 11), (3, 1, 11), (3, 8, 11), (3, 9, 11), (4, 11), (5, 9, 0),
    (5, 9, 1), (5, 8, 0), (5, 8, 1), (5, 1, 0), (5, 1, 1), (5, 11, 0),
)
SLOTS = len(SPOTS)
SHARED = len(LEFT)
NT = (((1,), (1,)), ((), ()))


def place():
    owner, z = lax.axis_index("owner"), lax.axis_index("rep")
    return owner // (2 * SIDE), (owner // 2) % SIDE, owner % 2, z


def at(here, step, flip):
    x, y, core, z = here
    x = (x + step[0] + SIDE) % SIDE
    y = (y + step[1] + SIDE) % SIDE
    z = (z + step[2] + SIDE) % SIDE
    return ((x * SIDE + y) * 2 + (core + flip) % 2, z)


def kernel(
    emb_ref, cluster_ref, out_ref, rows, names, results, near, held, tall, wide,
    row_send, row_recv, name_send, name_recv, pair_send, pair_recv, pname_send, pname_recv,
    result_send, result_recv,
):
    here = place()
    core = here[2]
    count = emb_ref.shape[0]
    part = count // CHUNKS

    barrier = pltpu.get_barrier_semaphore()
    for step in STEPS:
        pl.semaphore_signal(barrier, 1, device_id=at(here, step, 0), device_id_type=MESH)
    pl.semaphore_signal(barrier, 1, device_id=at(here, (0, 0, 0), 1), device_id_type=MESH)

    values = emb_ref[...].astype(jnp.float32)
    factor = lax.rsqrt(jnp.mean(values * values, axis=1, keepdims=True) + 1e-06)
    rows[0, 0] = (values * (factor * emb_ref.shape[1] ** (-0.5))).astype(jnp.bfloat16)
    names[0, 0] = jnp.broadcast_to(cluster_ref[...].astype(jnp.float32), names.shape[2:])
    pl.semaphore_wait(barrier, len(STEPS) + 1)

    def chunk_copy(src, dst, chunk, step):
        span = pl.ds(chunk * part, part)
        return pltpu.make_async_remote_copy(
            rows.at[src, 0, span], rows.at[dst, 0, span], row_send, row_recv.at[dst, chunk],
            device_id=at(here, step, 0), device_id_type=MESH)

    def name_copy(src, dst, step):
        return pltpu.make_async_remote_copy(
            names.at[src, 0], names.at[dst, 0], name_send, name_recv.at[dst],
            device_id=at(here, step, 0), device_id_type=MESH)

    def pair_copy(slot):
        return pltpu.make_async_remote_copy(
            rows.at[slot, 0], rows.at[slot, 1], pair_send, pair_recv.at[slot],
            device_id=at(here, (0, 0, 0), 1), device_id_type=MESH)

    def pair_name_copy(slot):
        return pltpu.make_async_remote_copy(
            names.at[slot, 0], names.at[slot, 1], pname_send, pname_recv.at[slot],
            device_id=at(here, (0, 0, 0), 1), device_id_type=MESH)

    def result_copy(slot, side):
        back = tuple(-v for v in SPOTS[slot])
        return pltpu.make_async_remote_copy(
            held.at[side, slot], results.at[side, slot], result_send, result_recv.at[side],
            device_id=at(here, back, side), device_id_type=MESH)

    def forward(slot, chunk):
        for who in range(2):
            kids = [k for k in ORDER[who][chunk] if PARENT[who][chunk][k] == slot]
            if not kids:
                continue

            @pl.when(core == who)
            def _():
                for k in kids:
                    step = STEPS[WAY[who][chunk][k]]
                    chunk_copy(slot, k, chunk, step).start()
                    if chunk == 0:
                        name_copy(slot, k, step).start()

    def share(slot):
        pair_copy(slot).start()
        pair_name_copy(slot).start()

    joined = set()

    def join(slot):
        if slot not in joined:
            joined.add(slot)
            pair_copy(slot).wait_recv()
            pair_name_copy(slot).wait_recv()

    def open_step(slot):
        near[...] = jnp.broadcast_to(names[slot, 0, 0:1, :], (128, count)).T
        tall[...] = jnp.full(tall.shape, -1.0, jnp.float32)

    def pair(a, b):
        left = near[...]
        best = tall[...]
        both = rows[a].reshape(2 * count, rows.shape[3])
        scores = lax.dot_general(rows[b, 0], both, NT, preferred_element_type=jnp.float32)
        for side in range(2):
            for half in range(count // 128):
                low = half * 128
                tile = scores[:, side * count + low:side * count + low + 128]
                match = left == names[a, side, 0:1, low:low + 128]
                if a == b and side == 0:
                    i = lax.broadcasted_iota(jnp.int32, tile.shape, 0)
                    j = lax.broadcasted_iota(jnp.int32, tile.shape, 1) + low
                    match = match & (i != j)
                tile = jnp.where(match, tile, jnp.float32(-1.0))
                best = jnp.maximum(best, tile)
                if a != b:
                    up = jnp.max(tile.reshape(count // 8, 8, 128), axis=0)
                    held[side, a, :, low:low + 128] = jnp.maximum(held[side, a, :, low:low + 128], up)
        tall[...] = best

    def close_step(slot):
        flat = tall[...].T
        held[0, slot] = jnp.max(flat.reshape(128 // 8, 8, count), axis=0)
        if slot < SHARED:
            held[1, slot] = jnp.full(held.shape[2:], -1.0, jnp.float32)

    for chunk in range(CHUNKS):
        forward(0, chunk)
    share(0)
    for task in TASKS:
        kind = task[0]
        if kind == 0:
            slot, chunk = task[1:]
            chunk_copy(0, slot, chunk, STEPS[0]).wait_recv()
            if chunk == 0:
                name_copy(0, slot, STEPS[0]).wait_recv()
            forward(slot, chunk)
        elif kind == 1:
            share(task[1])
        elif kind == 2:
            open_step(task[1])
        elif kind == 3:
            join(task[1])
            pair(task[1], task[2])
        elif kind == 4:
            close_step(task[1])
        else:
            result_copy(task[1], task[2]).start()

    pltpu.make_async_remote_copy(
        results.at[0, 1:SLOTS], results.at[0, 1:SLOTS], result_send, result_recv.at[0],
        device_id=at(here, STEPS[0], 0), device_id_type=MESH).wait_recv()
    pltpu.make_async_remote_copy(
        results.at[1, 0:SHARED], results.at[1, 0:SHARED], result_send, result_recv.at[1],
        device_id=at(here, STEPS[0], 0), device_id_type=MESH).wait_recv()
    top = held[0, 0]
    for slot in range(1, SLOTS):
        top = jnp.maximum(top, results[0, slot])
    for slot in range(SHARED):
        top = jnp.maximum(top, results[1, slot])
    out_ref[...] = jnp.max(top, axis=0, keepdims=True)

    def drain(ref, sem):
        pltpu.make_async_remote_copy(
            ref, ref, sem, sem, device_id=at(here, STEPS[0], 0), device_id_type=MESH).wait_send()

    drain(rows.at[1:SLOTS, 0], row_send)
    drain(names.at[1:SLOTS, 0], name_send)
    drain(rows.at[0:SHARED, 0], pair_send)
    drain(names.at[0:SHARED, 0], pname_send)
    drain(results.at[0, 1:SLOTS], result_send)
    drain(results.at[0, 0:SHARED], result_send)


def on_device(embeddings, cluster):
    count, width = embeddings.shape
    dma = pltpu.SemaphoreType.DMA
    best = pl.pallas_call(
        kernel,
        out_shape=jax.ShapeDtypeStruct((1, count), jnp.float32),
        in_specs=[pl.BlockSpec(memory_space=pltpu.VMEM)] * 2,
        out_specs=pl.BlockSpec(memory_space=pltpu.VMEM),
        scratch_shapes=[
            pltpu.VMEM((SLOTS, 2, count, width), jnp.bfloat16),
            pltpu.VMEM((SLOTS, 2, 8, count), jnp.float32),
            pltpu.VMEM((2, SLOTS, 8, count), jnp.float32),
            pltpu.VMEM((count, 128), jnp.float32),
            pltpu.VMEM((2, SLOTS, 8, count), jnp.float32),
            pltpu.VMEM((count, 128), jnp.float32),
            pltpu.VMEM((8, count), jnp.float32),
            dma(()), dma((SLOTS, CHUNKS)), dma(()), dma((SLOTS,)),
            dma(()), dma((SLOTS,)), dma(()), dma((SLOTS,)),
            dma(()), dma((2,)),
        ],
        compiler_params=pltpu.CompilerParams(
            collective_id=0, has_side_effects=True, vmem_limit_bytes=48 * 2**20),
    )(embeddings, cluster.reshape(1, count))
    return best.reshape(count)


def solution(mesh):
    return jax.shard_map(
        on_device,
        mesh=mesh,
        in_specs=(P(("owner", "rep"), None), P(("owner", "rep"))),
        out_specs=P(("owner", "rep")),
        check_vma=False,
    )
```

time: 195 us -> 52.2 us (0.27)
  waiting for transfers between devices: 82.6 us -> 0 us
  blocking collectives: 54.2 us -> 0 us
  Pallas kernels: 0 us -> 49.7 us
  matrix products: 27.1 us -> 0 us
  between operations: 13.5 us -> 0.01 us
  other arithmetic: 8.47 us -> 0 us
  starting transfers between devices: 4.14 us -> 0 us
  local copies, waits for them, and re-layouts: 4.36 us -> 2.28 us
    all_gather x1 -> x0, waiting for transfers between devices: 78.5 us -> none  [on_device(): lax.all_gather(members, 'owner', axis=0, tiled=True)]
    pallas_call x0 -> x1, Pallas kernels: none -> 49.7 us  [on_device(): pl.pallas_call(kernel, out_shape=jax.ShapeDtypeStruct((1, count), jnp.flo...]
    all_gather x1 -> x0, blocking collectives: 27.8 us -> none  [on_device(): lax.all_gather(member_meta, 'owner', axis=0, tiled=True)]
    dot_general x1 -> x0, matrix products: 27.1 us -> none  [masked_scores(): lax.dot_general(left, right, (((1,), (1,)), ((), ())), preferred_element_...]
    all_to_all x2 -> x0, blocking collectives: 26.4 us -> none  [the longest x1 19.9 us: on_device(): lax.all_to_all(outgoing.reshape(groups, capacity, width), 'rep', split_ax...]
    all_to_all x1 -> x0, starting transfers between devices: 4.13 us -> none  [on_device(): lax.all_to_all(best.reshape(groups, capacity), 'rep', split_axis=0, conca...]
    all_to_all x1 -> x0, waiting for transfers between devices: 4.1 us -> none  [on_device(): lax.all_to_all(best.reshape(groups, capacity), 'rep', split_axis=0, conca...]
    another operation x4 -> x0, other arithmetic: 2.56 us -> none
  transfers between devices with their start and end apart: 2 -> 0, of which waited for: 2 -> 0; matrix products, arithmetic and copies ran while one was open for 1% -> 0% of each run, Pallas kernels for 0% -> 0%
where the time goes in v1:
time: 52.2 us; the launch traced here: 52 us
  Pallas kernels  49.7 us (95%)
  local copies, waits for them, and re-layouts  2.28 us (4%)
    pallas_call x1, Pallas kernels, on_device(): pl.pallas_call(kernel, out_shape=jax.ShapeDtypeStruct((1, count), jnp.flo...  49.7 us
    unnamed x5, local copies, waits for them, and re-layouts  2.28 us

profile of v1, /device:TPU:1, one launch (start us, length us, event | category | flops | bytes accessed | tf_op | source)
XLA Modules:
  0.0 52.0 jit_solution(13683543452124397730)
XLA Ops:
  0.0 0.0 copy-start.1
  0.0 0.7 %copy-done.1 = s32[256]{0:T(256)S(1)} copy-done((s32[256]{0:T(256)S(1)}, s32[256]{0:T(256)}, u32[]{:S(2)}) %copy-start.1) | copy-done | bytes 1048
  0.7 0.0 copy-start
  0.7 1.0 %copy-done = bf16[256,1024]{1,0:T(8,128)(2,1)S(1)} copy-done((bf16[256,1024]{1,0:T(8,128)(2,1)S(1)}, bf16[256,1024]{1,0:T(8,128)(2,1)}, u32[]{:S(2)}) %copy-start) | copy-done | bytes 524312
  1.7 49.7 %shard_map.28 = f32[1,256]{1,0:T(1,128)S(1)} custom-call(bf16[256,1024]{1,0:T(8,128)(2,1)S(1)} %copy-done, s32[1,256]{1,0:T(1,128)S(1)} %bitcast.3), custom_call_target="tpu_custom_call" | custom-call | tf_op jit(solution)/shard_map/pallas_call | solution.py:259
  51.4 0.6 %copy.4 = f32[256]{0:T(256)} copy(f32[256]{0:T(256)S(1)} %bitcast.2) | data formatting | bytes 2048
Async XLA Ops:
  0.0 0.7 %copy-start.1 = (s32[256]{0:T(256)S(1)}, s32[256]{0:T(256)}, u32[]{:S(2)}) copy-start(s32[256]{0:T(256)} %param.3) | copy-start | bytes 3076
  0.7 1.0 %copy-start = (bf16[256,1024]{1,0:T(8,128)(2,1)S(1)}, bf16[256,1024]{1,0:T(8,128)(2,1)}, u32[]{:S(2)}) copy-start(bf16[256,1024]{1,0:T(8,128)(2,1)} %emb_ref.1) | copy-start | bytes 1572868

commit v2 on v0

v2 whole, which is shorter than its diff:
```python
import jax
import jax.numpy as jnp
from jax import lax
from jax.experimental import pallas as pl
from jax.experimental.pallas import tpu as pltpu
from jax.sharding import PartitionSpec as P

MESH = pl.DeviceIdType.MESH
SIDE = 4
HOME = (0, 0, 0)
STEPS = ((1, 0, 0), (-1, 0, 0), (0, 1, 0), (0, -1, 0), (0, 0, 1), (0, 0, -1))
SPOTS = (
    ((0, 0, 0), (1, 0, 0), (3, 0, 0), (0, 1, 0), (0, 1, 1), (1, 3, 0), (3, 1, 0), (1, 0, 3), (1, 3, 1), (1, 1, 3), (1, 3, 2), (1, 1, 2)),
    ((0, 0, 0), (0, 0, 3), (0, 0, 1), (0, 3, 0), (1, 0, 1), (3, 3, 0), (0, 3, 3), (3, 2, 0), (2, 0, 1), (1, 3, 3), (0, 2, 3), (2, 2, 0)),
)
SHARED = ((0, 1, 2, 3, 4, 5, 6, 7, 8), (0, 1, 2, 3, 4, 5, 7, 8, 9, 11))
PARENT = (
    (
        (-1, 0, 0, 0, 3, 1, 2, 1, 5, 7, 8, 9),
        (-1, 0, 0, 0, 3, 1, 2, 1, 5, 7, 8, 9),
        (-1, 0, 0, 0, 3, 1, 2, 1, 5, 7, 8, 9),
        (-1, 0, 0, 0, 3, 1, 3, 1, 5, 7, 8, 9),
    ),
    (
        (-1, 0, 0, 0, 2, 3, 3, 5, 4, 6, 6, 7),
        (-1, 0, 0, 0, 2, 3, 3, 5, 4, 6, 6, 7),
        (-1, 0, 0, 0, 2, 3, 3, 5, 4, 6, 6, 7),
        (-1, 0, 0, 0, 2, 3, 3, 5, 4, 6, 6, 7),
    ),
)
WAY = (
    (
        (-1, 0, 1, 2, 4, 3, 2, 5, 4, 2, 4, 5),
        (-1, 0, 1, 2, 4, 3, 2, 5, 4, 2, 4, 5),
        (-1, 0, 1, 2, 4, 3, 2, 5, 4, 2, 4, 5),
        (-1, 0, 1, 2, 4, 3, 1, 5, 4, 2, 4, 5),
    ),
    (
        (-1, 5, 4, 3, 0, 1, 5, 3, 0, 0, 3, 1),
        (-1, 5, 4, 3, 0, 1, 5, 3, 0, 0, 3, 1),
        (-1, 5, 4, 3, 0, 1, 5, 3, 0, 0, 3, 1),
        (-1, 5, 4, 3, 0, 1, 5, 3, 0, 0, 3, 1),
    ),
)
ORDER = (
    (
        (5, 1, 7, 11, 2, 6, 9, 10, 3, 8, 4),
        (8, 1, 4, 7, 2, 10, 5, 3, 9, 6, 11),
        (7, 1, 5, 8, 9, 6, 11, 2, 3, 10, 4),
        (9, 2, 3, 5, 4, 8, 1, 11, 7, 10, 6),
    ),
    (
        (5, 3, 7, 2, 4, 1, 6, 8, 10, 9, 11),
        (1, 11, 3, 9, 2, 8, 6, 4, 10, 5, 7),
        (3, 7, 1, 4, 5, 2, 6, 9, 10, 8, 11),
        (3, 1, 5, 2, 8, 9, 10, 11, 7, 4, 6),
    ),
)
TASKS = (
    (
        (1, 0, 0), (2, 0, 0), (3, 0, 0), (4, 0, 0), (0, 1, 0), (0, 2, 0), (0, 3, 0), (2, 12, 0), (4, 12, 0),
        (0, 1, 1), (0, 2, 1), (0, 3, 1), (0, 1, 2), (0, 2, 2), (0, 3, 2), (0, 1, 3), (1, 1, 1), (0, 2, 3),
        (1, 2, 2), (0, 3, 3), (1, 3, 3), (2, 1, 0), (3, 12, 1), (3, 0, 1), (4, 1, 0), (2, 2, 0), (3, 12, 2),
        (3, 1, 2), (4, 2, 0), (0, 4, 0), (0, 5, 0), (0, 6, 0), (0, 7, 0), (2, 3, 0), (3, 12, 3), (3, 1, 3),
        (3, 0, 3), (3, 2, 3), (4, 3, 0), (0, 4, 1), (0, 5, 1), (0, 6, 1), (2, 13, 0), (3, 1, 13), (4, 13, 0),
        (2, 14, 0), (3, 2, 14), (4, 14, 0), (2, 15, 0), (3, 1, 15), (4, 15, 0), (0, 4, 2), (0, 5, 2),
        (0, 6, 2), (0, 7, 1), (0, 4, 3), (1, 4, 4), (0, 5, 3), (1, 5, 5), (0, 6, 3), (1, 6, 6), (2, 4, 0),
        (3, 1, 4), (3, 3, 4), (0, 9, 0), (3, 2, 4), (3, 13, 4), (3, 0, 4), (3, 15, 4), (4, 4, 0), (0, 7, 2),
        (0, 8, 0), (2, 5, 0), (3, 12, 5), (3, 3, 5), (3, 13, 5), (3, 14, 5), (3, 4, 5), (4, 5, 0), (5, 12, 0),
        (0, 8, 1), (2, 6, 0), (3, 1, 6), (3, 13, 6), (0, 9, 1), (3, 4, 6), (3, 15, 6), (3, 5, 6), (4, 6, 0),
        (5, 1, 0), (0, 7, 3), (1, 7, 7), (0, 8, 2), (2, 16, 0), (3, 5, 16), (3, 6, 16), (4, 16, 0),
        (2, 17, 0), (4, 17, 0), (2, 7, 0), (3, 4, 7), (0, 8, 3), (1, 8, 8), (3, 16, 7), (3, 14, 7), (3, 5, 7),
        (0, 9, 2), (3, 2, 7), (3, 15, 7), (3, 0, 7), (3, 6, 7), (4, 7, 0), (0, 10, 0), (0, 11, 0), (2, 8, 0),
        (3, 7, 8), (3, 16, 8), (3, 13, 8), (3, 2, 8), (3, 3, 8), (0, 10, 1), (0, 11, 1), (3, 0, 8), (3, 6, 8),
        (3, 17, 8), (4, 8, 0), (5, 7, 0), (5, 16, 0), (5, 13, 0), (0, 9, 3), (2, 9, 0), (3, 4, 9), (3, 8, 9),
        (0, 10, 2), (3, 14, 9), (3, 0, 9), (3, 5, 9), (3, 15, 9), (4, 9, 0), (5, 4, 0), (5, 8, 0), (5, 14, 0),
        (0, 11, 2), (0, 10, 3), (2, 18, 0), (3, 9, 18), (4, 18, 0), (2, 19, 0), (3, 9, 19), (4, 19, 0),
        (5, 9, 0), (5, 19, 0), (2, 10, 0), (3, 2, 10), (3, 3, 10), (3, 5, 10), (3, 6, 10), (3, 17, 10),
        (3, 18, 10), (4, 10, 0), (5, 2, 0), (5, 3, 0), (5, 5, 0), (0, 11, 3), (2, 20, 0), (4, 20, 0),
        (2, 11, 0), (3, 0, 11), (3, 6, 11), (3, 10, 11), (3, 20, 11), (3, 15, 11), (3, 17, 11), (3, 18, 11),
        (4, 11, 0), (5, 6, 0), (5, 10, 0), (5, 20, 0), (5, 15, 0), (5, 17, 0), (5, 18, 0), (2, 21, 0),
        (3, 11, 21), (4, 21, 0), (5, 11, 0), (5, 21, 0),
    ),
    (
        (1, 0, 0), (2, 0, 0), (3, 0, 0), (4, 0, 0), (0, 1, 0), (0, 2, 0), (0, 3, 0), (2, 12, 0), (3, 0, 12),
        (4, 12, 0), (0, 1, 1), (0, 2, 1), (0, 3, 1), (0, 1, 2), (0, 2, 2), (0, 3, 2), (0, 1, 3), (1, 1, 1),
        (0, 2, 3), (1, 2, 2), (0, 3, 3), (1, 3, 3), (2, 1, 0), (3, 12, 1), (3, 0, 1), (4, 1, 0), (2, 2, 0),
        (3, 12, 2), (3, 1, 2), (4, 2, 0), (5, 12, 0), (0, 4, 0), (0, 5, 0), (2, 3, 0), (3, 0, 3), (3, 2, 3),
        (3, 1, 3), (4, 3, 0), (0, 4, 1), (0, 5, 1), (0, 6, 0), (2, 13, 0), (3, 2, 13), (4, 13, 0), (2, 14, 0),
        (3, 3, 14), (3, 1, 14), (4, 14, 0), (0, 4, 2), (0, 5, 2), (2, 15, 0), (3, 3, 15), (3, 1, 15),
        (3, 2, 15), (4, 15, 0), (0, 4, 3), (1, 4, 4), (0, 6, 1), (2, 4, 0), (3, 14, 4), (3, 3, 4), (3, 15, 4),
        (3, 0, 4), (3, 1, 4), (3, 2, 4), (4, 4, 0), (5, 14, 0), (0, 5, 3), (1, 5, 5), (0, 7, 0), (0, 8, 0),
        (2, 5, 0), (3, 15, 5), (3, 13, 5), (3, 4, 5), (3, 0, 5), (3, 1, 5), (4, 5, 0), (0, 6, 2), (0, 9, 0),
        (0, 10, 0), (2, 16, 0), (3, 5, 16), (4, 16, 0), (2, 17, 0), (3, 5, 17), (4, 17, 0), (2, 18, 0),
        (4, 18, 0), (0, 7, 1), (0, 8, 1), (0, 6, 3), (0, 7, 2), (0, 8, 2), (2, 6, 0), (3, 5, 6), (3, 13, 6),
        (0, 11, 0), (3, 4, 6), (3, 18, 6), (3, 16, 6), (3, 2, 6), (4, 6, 0), (0, 9, 1), (0, 10, 1),
        (2, 19, 0), (4, 19, 0), (0, 7, 3), (1, 7, 6), (0, 8, 3), (1, 8, 7), (2, 20, 0), (4, 20, 0), (2, 7, 0),
        (3, 13, 7), (0, 11, 1), (3, 4, 7), (3, 20, 7), (3, 19, 7), (0, 9, 2), (0, 10, 2), (3, 0, 7),
        (3, 1, 7), (3, 2, 7), (4, 7, 0), (5, 13, 0), (0, 11, 2), (2, 8, 0), (3, 5, 8), (3, 6, 8), (0, 9, 3),
        (1, 9, 8), (0, 10, 3), (3, 20, 8), (3, 17, 8), (3, 19, 8), (3, 0, 8), (3, 1, 8), (3, 2, 8), (4, 8, 0),
        (5, 5, 0), (5, 6, 0), (5, 20, 0), (5, 17, 0), (2, 9, 0), (3, 7, 9), (3, 1, 9), (3, 2, 9), (3, 18, 9),
        (0, 11, 3), (1, 11, 9), (3, 16, 9), (4, 9, 0), (5, 7, 0), (2, 10, 0), (3, 1, 10), (3, 2, 10),
        (3, 4, 10), (3, 8, 10), (3, 18, 10), (3, 0, 10), (3, 15, 10), (3, 16, 10), (4, 10, 0), (5, 1, 0),
        (5, 2, 0), (5, 4, 0), (5, 8, 0), (5, 18, 0), (5, 10, 0), (2, 11, 0), (3, 0, 11), (3, 3, 11),
        (3, 9, 11), (3, 15, 11), (3, 16, 11), (3, 19, 11), (4, 11, 0), (5, 3, 0), (5, 9, 0), (5, 15, 0),
        (5, 16, 0), (5, 19, 0), (5, 11, 0),
    ),
)
SLOTS = len(SPOTS[0])
TAKEN = max(len(shared) for shared in SHARED)
NODES = SLOTS + TAKEN
CHUNKS = len(PARENT[0])
NT = (((1,), (1,)), ((), ()))


def place():
    owner, z = lax.axis_index("owner"), lax.axis_index("rep")
    return owner // (2 * SIDE), (owner // 2) % SIDE, owner % 2, z


def kernel(
    emb_ref, cluster_ref, out_ref, raw, label, rows, names, held, leaving, results, near, tall,
    load_sem, row_send, row_recv, name_send, name_recv, pair_send, pair_recv,
    pname_send, pname_recv, result_send, result_recv,
):
    x, y, core, z = place()
    count = raw.shape[0]
    part = count // CHUNKS

    def at(step, flip):
        dx, dy, dz = step
        spot = ((x + dx + SIDE) % SIDE * SIDE + (y + dy + SIDE) % SIDE) * 2 + (core + flip) % 2
        return spot, (z + dz + SIDE) % SIDE

    loads = (
        pltpu.make_async_copy(emb_ref, raw, load_sem.at[0]),
        pltpu.make_async_copy(cluster_ref, label, load_sem.at[1]),
    )
    for load in loads:
        load.start()
    barrier = pltpu.get_barrier_semaphore()
    near_by = [at(step, 0) for step in STEPS]
    twin = at(HOME, 1)
    for spot in near_by + [twin]:
        pl.semaphore_signal(barrier, 1, device_id=spot, device_id_type=MESH)
    for load in loads:
        load.wait()

    values = raw[...].astype(jnp.float32)
    factor = lax.rsqrt(jnp.mean(values * values, axis=1, keepdims=True) + 1e-06)
    rows[0] = (values * (factor * raw.shape[1] ** (-0.5))).astype(jnp.bfloat16)
    names[0] = jnp.broadcast_to(label[...].astype(jnp.float32), names.shape[1:])
    pl.semaphore_wait(barrier, len(STEPS) + 1)

    def remote(src, dst, send, recv, spot):
        return pltpu.make_async_remote_copy(
            src, dst, send, recv, device_id=spot, device_id_type=MESH)

    def chunk_copy(src, dst, chunk, spot):
        span = pl.ds(chunk * part, part)
        return remote(rows.at[src, span], rows.at[dst, span], row_send, row_recv.at[dst, chunk], spot)

    def name_copy(src, dst, spot):
        return remote(names.at[src], names.at[dst], name_send, name_recv.at[dst], spot)

    def pair_copy(slot, i):
        return remote(rows.at[slot], rows.at[SLOTS + i], pair_send, pair_recv.at[i], twin)

    def pair_name_copy(slot, i):
        return remote(names.at[slot], names.at[SLOTS + i], pname_send, pname_recv.at[i], twin)

    def result_copy(who, node):
        flip = int(node >= SLOTS)
        spot = SPOTS[1 - who][SHARED[1 - who][node - SLOTS]] if flip else SPOTS[who][node]
        return remote(leaving.at[node], results.at[node], result_send, result_recv.at[flip],
                      at(tuple(-v for v in spot), flip))

    def forward(who, slot, chunk):
        for k in ORDER[who][chunk]:
            if PARENT[who][chunk][k] == slot:
                spot = near_by[WAY[who][chunk][k]]
                chunk_copy(slot, k, chunk, spot).start()
                if chunk == 0:
                    name_copy(slot, k, spot).start()

    def open_step(b):
        near[...] = jnp.broadcast_to(names[b, 0:1, :], (128, count)).T
        tall[...] = jnp.full(tall.shape, -1.0, jnp.float32)

    def pair(a, b):
        left = near[...]
        best = tall[...]
        scores = lax.dot_general(rows[b], rows[a], NT, preferred_element_type=jnp.float32)
        for low in range(0, count, 128):
            tile = scores[:, low:low + 128]
            match = left == names[a, 0:1, low:low + 128]
            if a == b:
                i = lax.broadcasted_iota(jnp.int32, tile.shape, 0)
                j = lax.broadcasted_iota(jnp.int32, tile.shape, 1) + low
                match = match & (i != j)
            tile = jnp.where(match, tile, jnp.float32(-1.0))
            best = jnp.maximum(best, tile)
            if a != b:
                up = jnp.max(tile.reshape(count // 8, 8, 128), axis=0)
                held[a, :, low:low + 128] = jnp.maximum(held[a, :, low:low + 128], up)
        tall[...] = best

    def close_step(b):
        held[b] = jnp.max(tall[...].T.reshape(128 // 8, 8, count), axis=0)

    def program(who):
        for chunk in range(CHUNKS):
            forward(who, 0, chunk)
        for kind, one, two in TASKS[who]:
            if kind == 0:
                chunk_copy(0, one, two, twin).wait_recv()
                if two == 0:
                    name_copy(0, one, twin).wait_recv()
                forward(who, one, two)
            elif kind == 1:
                pair_copy(one, two).start()
                pair_name_copy(one, two).start()
            elif kind == 2:
                if one >= SLOTS:
                    pair_copy(0, one - SLOTS).wait_recv()
                    pair_name_copy(0, one - SLOTS).wait_recv()
                open_step(one)
            elif kind == 3:
                pair(one, two)
            elif kind == 4:
                close_step(one)
            else:
                leaving[one] = jnp.max(held[one], axis=0, keepdims=True)
                result_copy(who, one).start()

        given, taken = len(SHARED[who]), len(SHARED[1 - who])
        own, other = results.at[1:SLOTS], results.at[SLOTS:SLOTS + given]
        remote(own, own, result_send, result_recv.at[0], twin).wait_recv()
        remote(other, other, result_send, result_recv.at[1], twin).wait_recv()
        top = jnp.max(held[0], axis=0, keepdims=True)
        for node in range(1, SLOTS + given):
            top = jnp.maximum(top, results[node])
        out_ref[...] = top

        def drain(ref, sem):
            remote(ref, ref, sem, sem, twin).wait_send()

        drain(rows.at[1:SLOTS], row_send)
        drain(names.at[1:SLOTS], name_send)
        drain(rows.at[0:given], pair_send)
        drain(names.at[0:given], pname_send)
        drain(results.at[1:SLOTS + taken], result_send)

    for who in range(2):
        pl.when(core == who)(lambda who=who: program(who))


def on_device(embeddings, cluster):
    count, width = embeddings.shape
    dma = pltpu.SemaphoreType.DMA
    best = pl.pallas_call(
        kernel,
        out_shape=jax.ShapeDtypeStruct((1, count), jnp.float32),
        in_specs=[pl.BlockSpec(memory_space=pl.ANY)] * 2,
        out_specs=pl.BlockSpec(memory_space=pltpu.VMEM),
        scratch_shapes=[
            pltpu.VMEM((count, width), jnp.bfloat16),
            pltpu.VMEM((1, count), jnp.int32),
            pltpu.VMEM((NODES, count, width), jnp.bfloat16),
            pltpu.VMEM((NODES, 8, count), jnp.float32),
            pltpu.VMEM((NODES, 8, count), jnp.float32),
            pltpu.VMEM((NODES, 1, count), jnp.float32),
            pltpu.VMEM((NODES, 1, count), jnp.float32),
            pltpu.VMEM((count, 128), jnp.float32),
            pltpu.VMEM((count, 128), jnp.float32),
            dma((2,)), dma(()), dma((SLOTS, CHUNKS)), dma(()), dma((SLOTS,)),
            dma(()), dma((TAKEN,)), dma(()), dma((TAKEN,)),
            dma(()), dma((2,)),
        ],
        compiler_params=pltpu.CompilerParams(
            collective_id=0, has_side_effects=True, vmem_limit_bytes=56 * 2**20),
    )(embeddings, cluster.reshape(1, count))
    return best.reshape(count)


def solution(mesh):
    return jax.shard_map(
        on_device,
        mesh=mesh,
        in_specs=(P(("owner", "rep"), None), P(("owner", "rep"))),
        out_specs=P(("owner", "rep")),
        check_vma=False,
    )
```

time: 195 us -> 47 us (0.24)
  waiting for transfers between devices: 82.6 us -> 0 us
  blocking collectives: 54.2 us -> 0 us
  Pallas kernels: 0 us -> 45.7 us
  matrix products: 27.1 us -> 0 us
  between operations: 13.5 us -> 0.02 us
  other arithmetic: 8.47 us -> 0 us
  starting transfers between devices: 4.14 us -> 0 us
  local copies, waits for them, and re-layouts: 4.36 us -> 1.22 us
    all_gather x1 -> x0, waiting for transfers between devices: 78.5 us -> none  [on_device(): lax.all_gather(members, 'owner', axis=0, tiled=True)]
    pallas_call x0 -> x1, Pallas kernels: none -> 45.7 us  [on_device(): pl.pallas_call(kernel, out_shape=jax.ShapeDtypeStruct((1, count), jnp.flo...]
    all_gather x1 -> x0, blocking collectives: 27.8 us -> none  [on_device(): lax.all_gather(member_meta, 'owner', axis=0, tiled=True)]
    dot_general x1 -> x0, matrix products: 27.1 us -> none  [masked_scores(): lax.dot_general(left, right, (((1,), (1,)), ((), ())), preferred_element_...]
    all_to_all x2 -> x0, blocking collectives: 26.4 us -> none  [the longest x1 19.9 us: on_device(): lax.all_to_all(outgoing.reshape(groups, capacity, width), 'rep', split_ax...]
    all_to_all x1 -> x0, starting transfers between devices: 4.13 us -> none  [on_device(): lax.all_to_all(best.reshape(groups, capacity), 'rep', split_axis=0, conca...]
    all_to_all x1 -> x0, waiting for transfers between devices: 4.1 us -> none  [on_device(): lax.all_to_all(best.reshape(groups, capacity), 'rep', split_axis=0, conca...]
    another operation x4 -> x0, other arithmetic: 2.56 us -> none
  transfers between devices with their start and end apart: 2 -> 0, of which waited for: 2 -> 0; matrix products, arithmetic and copies ran while one was open for 1% -> 0% of each run, Pallas kernels for 0% -> 0%
where the time goes in v2:
time: 47 us; the launch traced here: 46.9 us
  Pallas kernels  45.7 us (97%)
  local copies, waits for them, and re-layouts  1.22 us (3%)
    pallas_call x1, Pallas kernels, on_device(): pl.pallas_call(kernel, out_shape=jax.ShapeDtypeStruct((1, count), jnp.flo...  45.7 us
    unnamed x3, local copies, waits for them, and re-layouts  1.22 us

profile of v2, /device:TPU:1, one launch (start us, length us, event | category | flops | bytes accessed | tf_op | source)
XLA Modules:
  0.0 46.9 jit_solution(64244726256965319)
XLA Ops:
  0.0 45.7 %shard_map.28 = f32[1,256]{1,0:T(1,128)} custom-call(bf16[256,1024]{1,0:T(8,128)(2,1)} %emb_ref.1, s32[1,256]{1,0:T(1,128)} %bitcast.3), custom_call_target="tpu_custom_call" | custom-call | tf_op jit(solution)/shard_map/pallas_call | solution.py:261
  45.7 0.0 copy-start
  45.7 0.7 %copy-done = f32[1,256]{1,0:T(1,128)S(1)} copy-done((f32[1,256]{1,0:T(1,128)S(1)}, f32[1,256]{1,0:T(1,128)}, u32[]{:S(2)}) %copy-start) | copy-done | bytes 1048
  46.3 0.6 %copy.4 = f32[256]{0:T(256)} copy(f32[256]{0:T(256)S(1)} %bitcast.2) | data formatting | bytes 2048
Async XLA Ops:
  45.7 0.7 %copy-start = (f32[1,256]{1,0:T(1,128)S(1)}, f32[1,256]{1,0:T(1,128)}, u32[]{:S(2)}) copy-start(f32[1,256]{1,0:T(1,128)} %shard_map.28) | copy-start | bytes 3076

commit v3 on v2

v3 whole, which is shorter than its diff:
```python
import jax
import jax.numpy as jnp
from jax import lax
from jax.experimental import pallas as pl
from jax.experimental.pallas import tpu as pltpu
from jax.sharding import PartitionSpec as P

MESH = pl.DeviceIdType.MESH
SIDE = 4
HOME = (0, 0, 0)
STEPS = ((1, 0, 0), (-1, 0, 0), (0, 1, 0), (0, -1, 0), (0, 0, 1), (0, 0, -1))
SPOTS = (
    ((0, 0, 0), (1, 0, 0), (3, 0, 0), (0, 1, 0), (0, 0, 1), (0, 1, 3), (3, 3, 0), (0, 2, 3), (0, 0, 2), (2, 0, 0), (0, 2, 2), (2, 3, 0)),
    ((0, 0, 0), (0, 0, 3), (0, 3, 0), (1, 3, 0), (0, 1, 3), (2, 3, 0), (3, 3, 0), (0, 3, 1), (0, 1, 2), (2, 2, 0), (0, 3, 2), (3, 2, 0)),
)
SHARED = ((0, 1, 2, 3, 4, 5, 6, 7, 8), (0, 1, 2, 3, 4, 5, 6, 7, 8, 9, 11))
PARENT = (
    (
        (-1, 0, 0, 0, 0, 3, 2, 5, 4, 2, 7, 6),
        (-1, 0, 0, 0, 0, 3, 2, 5, 4, 2, 7, 6),
        (-1, 0, 0, 0, 0, 3, 2, 5, 4, 2, 7, 6),
        (-1, 0, 0, 0, 0, 3, 2, 5, 4, 2, 7, 6),
    ),
    (
        (-1, 0, 0, 2, 1, 6, 2, 2, 4, 11, 7, 6),
        (-1, 0, 0, 2, 1, 3, 2, 2, 4, 5, 7, 6),
        (-1, 0, 0, 2, 1, 3, 2, 2, 4, 5, 7, 6),
        (-1, 0, 0, 2, 1, 3, 2, 2, 4, 5, 7, 6),
    ),
)
WAY = (
    (
        (-1, 0, 1, 2, 4, 5, 3, 2, 4, 1, 5, 1),
        (-1, 0, 1, 2, 4, 5, 3, 2, 4, 1, 5, 1),
        (-1, 0, 1, 2, 4, 5, 3, 2, 4, 1, 5, 1),
        (-1, 0, 1, 2, 4, 5, 3, 2, 4, 1, 5, 1),
    ),
    (
        (-1, 5, 3, 0, 2, 1, 1, 4, 5, 1, 4, 3),
        (-1, 5, 3, 0, 2, 0, 1, 4, 5, 3, 4, 3),
        (-1, 5, 3, 0, 2, 0, 1, 4, 5, 3, 4, 3),
        (-1, 5, 3, 0, 2, 0, 1, 4, 5, 3, 4, 3),
    ),
)
ORDER = (
    (
        (2, 8, 9, 1, 7, 4, 11, 5, 6, 10, 3),
        (3, 10, 11, 2, 4, 7, 1, 5, 6, 9, 8),
        (9, 5, 1, 3, 11, 7, 10, 2, 8, 4, 6),
        (7, 5, 8, 11, 3, 1, 6, 2, 4, 9, 10),
    ),
    (
        (11, 4, 2, 10, 5, 9, 1, 8, 3, 6, 7),
        (2, 3, 10, 9, 8, 4, 1, 5, 7, 11, 6),
        (11, 5, 3, 9, 7, 2, 6, 8, 10, 1, 4),
        (8, 2, 11, 1, 9, 7, 6, 4, 3, 10, 5),
    ),
)
TASKS = (
    (
        (1, 0, 0), (2, 0, 0), (3, 0, 0), (4, 0, 0), (0, 2, 0), (0, 3, 0), (0, 4, 0), (2, 12, 0), (4, 12, 0),
        (0, 2, 1), (0, 3, 1), (0, 4, 1), (0, 2, 2), (0, 3, 2), (0, 4, 2), (0, 5, 0), (0, 6, 0), (0, 2, 3),
        (0, 3, 3), (0, 4, 3), (0, 1, 0), (0, 1, 1), (0, 1, 2), (0, 1, 3), (1, 1, 1), (2, 1, 0), (3, 0, 1),
        (1, 2, 2), (1, 3, 3), (1, 4, 4), (3, 12, 1), (4, 1, 0), (2, 2, 0), (3, 12, 2), (0, 5, 1), (0, 6, 1),
        (3, 1, 2), (4, 2, 0), (2, 3, 0), (3, 0, 3), (3, 2, 3), (3, 1, 3), (4, 3, 0), (2, 4, 0), (3, 0, 4),
        (0, 5, 2), (0, 6, 2), (3, 12, 4), (3, 2, 4), (3, 3, 4), (3, 1, 4), (4, 4, 0), (2, 13, 0), (3, 2, 13),
        (3, 3, 13), (3, 4, 13), (3, 1, 13), (4, 13, 0), (2, 14, 0), (3, 2, 14), (0, 7, 0), (3, 3, 14),
        (3, 1, 14), (4, 14, 0), (0, 5, 3), (0, 6, 3), (1, 5, 5), (2, 5, 0), (3, 2, 5), (1, 6, 6), (3, 12, 5),
        (0, 7, 1), (3, 14, 5), (3, 1, 5), (3, 4, 5), (4, 5, 0), (5, 2, 0), (2, 6, 0), (3, 12, 6), (3, 3, 6),
        (3, 13, 6), (0, 7, 2), (3, 1, 6), (3, 5, 6), (3, 4, 6), (4, 6, 0), (5, 12, 0), (2, 15, 0), (3, 5, 15),
        (3, 6, 15), (4, 15, 0), (2, 16, 0), (3, 6, 16), (4, 16, 0), (0, 7, 3), (1, 7, 7), (2, 7, 0),
        (3, 0, 7), (0, 8, 0), (0, 8, 1), (0, 8, 2), (0, 8, 3), (1, 8, 8), (3, 14, 7), (3, 15, 7), (3, 4, 7),
        (3, 1, 7), (3, 6, 7), (4, 7, 0), (2, 8, 0), (3, 0, 8), (3, 14, 8), (3, 15, 8), (3, 1, 8), (3, 5, 8),
        (3, 6, 8), (3, 13, 8), (4, 8, 0), (5, 15, 0), (5, 14, 0), (2, 17, 0), (3, 7, 17), (3, 8, 17),
        (4, 17, 0), (5, 17, 0), (2, 18, 0), (3, 7, 18), (3, 8, 18), (4, 18, 0), (5, 18, 0), (2, 19, 0),
        (4, 19, 0), (0, 9, 0), (0, 9, 1), (0, 9, 2), (0, 9, 3), (2, 9, 0), (3, 5, 9), (3, 7, 9), (3, 13, 9),
        (3, 19, 9), (3, 16, 9), (3, 4, 9), (3, 8, 9), (4, 9, 0), (5, 7, 0), (5, 5, 0), (5, 16, 0), (5, 19, 0),
        (5, 13, 0), (2, 20, 0), (3, 9, 20), (4, 20, 0), (5, 20, 0), (0, 10, 0), (0, 10, 1), (0, 10, 2),
        (0, 10, 3), (2, 10, 0), (3, 1, 10), (3, 6, 10), (3, 9, 10), (3, 8, 10), (4, 10, 0), (5, 6, 0),
        (5, 9, 0), (5, 1, 0), (2, 21, 0), (3, 10, 21), (4, 21, 0), (5, 21, 0), (2, 22, 0), (3, 10, 22),
        (4, 22, 0), (5, 10, 0), (5, 22, 0), (0, 11, 0), (0, 11, 1), (0, 11, 2), (0, 11, 3), (2, 11, 0),
        (3, 3, 11), (3, 4, 11), (3, 8, 11), (4, 11, 0), (5, 11, 0), (5, 8, 0), (5, 3, 0), (5, 4, 0),
    ),
    (
        (1, 0, 0), (2, 0, 0), (3, 0, 0), (4, 0, 0), (0, 1, 0), (0, 2, 0), (2, 12, 0), (3, 0, 12), (4, 12, 0),
        (0, 1, 1), (0, 2, 1), (0, 1, 2), (0, 2, 2), (0, 4, 0), (0, 6, 0), (0, 7, 0), (0, 1, 3), (0, 2, 3),
        (1, 1, 1), (2, 1, 0), (3, 0, 1), (4, 1, 0), (1, 2, 2), (2, 2, 0), (3, 12, 2), (0, 3, 1), (0, 4, 1),
        (3, 0, 2), (3, 1, 2), (4, 2, 0), (0, 6, 1), (0, 7, 1), (2, 13, 0), (4, 13, 0), (2, 14, 0), (4, 14, 0),
        (0, 3, 2), (0, 4, 2), (2, 15, 0), (4, 15, 0), (2, 16, 0), (4, 16, 0), (0, 3, 3), (0, 6, 2), (0, 7, 2),
        (0, 3, 0), (1, 3, 3), (2, 3, 0), (3, 14, 3), (0, 11, 0), (3, 2, 3), (0, 4, 3), (3, 0, 3), (3, 1, 3),
        (0, 5, 1), (3, 15, 3), (3, 16, 3), (4, 3, 0), (1, 4, 4), (2, 4, 0), (3, 12, 4), (3, 2, 4), (3, 13, 4),
        (3, 3, 4), (0, 5, 2), (3, 16, 4), (4, 4, 0), (5, 12, 0), (2, 17, 0), (4, 17, 0), (2, 18, 0),
        (4, 18, 0), (0, 5, 3), (0, 5, 0), (1, 5, 5), (2, 5, 0), (3, 2, 5), (0, 6, 3), (0, 7, 3), (3, 0, 5),
        (3, 1, 5), (3, 16, 5), (3, 15, 5), (1, 6, 6), (1, 7, 7), (3, 17, 5), (3, 4, 5), (4, 5, 0), (2, 6, 0),
        (3, 0, 6), (3, 1, 6), (3, 16, 6), (0, 8, 0), (0, 8, 1), (0, 8, 2), (0, 8, 3), (1, 8, 8), (3, 15, 6),
        (3, 17, 6), (3, 4, 6), (4, 6, 0), (2, 7, 0), (3, 6, 7), (3, 1, 7), (3, 17, 7), (3, 13, 7), (3, 14, 7),
        (3, 4, 7), (3, 3, 7), (3, 5, 7), (3, 18, 7), (4, 7, 0), (5, 6, 0), (0, 9, 1), (0, 9, 2), (0, 9, 0),
        (0, 9, 3), (1, 9, 9), (2, 8, 0), (3, 13, 8), (3, 14, 8), (3, 3, 8), (3, 5, 8), (3, 18, 8), (4, 8, 0),
        (5, 13, 0), (5, 14, 0), (2, 19, 0), (4, 19, 0), (0, 11, 1), (0, 11, 2), (0, 11, 3), (1, 11, 10),
        (2, 20, 0), (3, 8, 20), (4, 20, 0), (2, 9, 0), (3, 0, 9), (3, 4, 9), (3, 19, 9), (3, 16, 9),
        (3, 20, 9), (3, 15, 9), (3, 8, 9), (4, 9, 0), (5, 9, 0), (0, 10, 0), (0, 10, 1), (0, 10, 2),
        (0, 10, 3), (2, 10, 0), (3, 1, 10), (3, 2, 10), (3, 3, 10), (3, 5, 10), (3, 17, 10), (3, 18, 10),
        (3, 8, 10), (4, 10, 0), (5, 5, 0), (5, 3, 0), (5, 17, 0), (5, 18, 0), (5, 1, 0), (5, 2, 0),
        (2, 11, 0), (3, 0, 11), (3, 4, 11), (3, 7, 11), (3, 8, 11), (3, 10, 11), (3, 19, 11), (3, 16, 11),
        (3, 20, 11), (3, 15, 11), (4, 11, 0), (5, 8, 0), (5, 10, 0), (5, 11, 0), (5, 19, 0), (5, 4, 0),
        (5, 7, 0), (5, 20, 0), (5, 15, 0), (5, 16, 0),
    ),
)
SLOTS = len(SPOTS[0])
TAKEN = max(len(shared) for shared in SHARED)
NODES = SLOTS + TAKEN
CHUNKS = len(PARENT[0])
NT = (((1,), (1,)), ((), ()))


def place():
    owner, z = lax.axis_index("owner"), lax.axis_index("rep")
    return owner // (2 * SIDE), (owner // 2) % SIDE, owner % 2, z


def kernel(
    emb_ref, cluster_ref, out_ref, raw, label, rows, names, held, leaving, results, near, tall,
    load_sem, row_send, row_recv, name_send, name_recv, pair_send, pair_recv,
    pname_send, pname_recv, result_send, result_recv,
):
    x, y, core, z = place()
    count = raw.shape[0]
    part = count // CHUNKS

    def wrap(v):
        return jnp.where(v >= SIDE, v - SIDE, v)

    def at(step, flip):
        nx, ny, nz = (wrap(v + d % SIDE) for v, d in zip((x, y, z), step))
        return (nx * SIDE + ny) * 2 + (1 - core if flip else core), nz

    loads = (
        pltpu.make_async_copy(emb_ref, raw, load_sem.at[0]),
        pltpu.make_async_copy(cluster_ref, label, load_sem.at[1]),
    )
    for load in loads:
        load.start()
    barrier = pltpu.get_barrier_semaphore()
    near_by = [at(step, 0) for step in STEPS]
    twin = at(HOME, 1)
    for spot in near_by + [twin]:
        pl.semaphore_signal(barrier, 1, device_id=spot, device_id_type=MESH)
    homes = [[
        at(tuple(-v for v in SPOTS[who][node]), 0) if node < SLOTS else
        at(tuple(-v for v in SPOTS[1 - who][SHARED[1 - who][node - SLOTS]]), 1)
        for node in range(SLOTS + len(SHARED[1 - who]))] for who in range(2)]
    for load in loads:
        load.wait()

    values = raw[...].astype(jnp.float32)
    factor = lax.rsqrt(jnp.mean(values * values, axis=1, keepdims=True) + 1e-06)
    rows[0] = (values * (factor * raw.shape[1] ** (-0.5))).astype(jnp.bfloat16)
    names[0] = jnp.broadcast_to(label[...].astype(jnp.float32), names.shape[1:])
    pl.semaphore_wait(barrier, len(STEPS) + 1)

    def remote(src, dst, send, recv, spot):
        return pltpu.make_async_remote_copy(
            src, dst, send, recv, device_id=spot, device_id_type=MESH)

    def chunk_copy(src, dst, chunk, spot):
        span = pl.ds(chunk * part, part)
        return remote(rows.at[src, span], rows.at[dst, span], row_send, row_recv.at[dst, chunk], spot)

    def name_copy(src, dst, spot):
        return remote(names.at[src], names.at[dst], name_send, name_recv.at[dst], spot)

    def pair_copy(slot, i):
        return remote(rows.at[slot], rows.at[SLOTS + i], pair_send, pair_recv.at[i], twin)

    def pair_name_copy(slot, i):
        return remote(names.at[slot], names.at[SLOTS + i], pname_send, pname_recv.at[i], twin)

    def result_copy(who, node):
        flip = int(node >= SLOTS)
        return remote(leaving.at[node], results.at[node], result_send, result_recv.at[flip],
                      homes[who][node])

    def forward(who, slot, chunk):
        for k in ORDER[who][chunk]:
            if PARENT[who][chunk][k] == slot:
                spot = near_by[WAY[who][chunk][k]]
                chunk_copy(slot, k, chunk, spot).start()
                if chunk == 0:
                    name_copy(slot, k, spot).start()

    def open_step(b):
        near[...] = jnp.broadcast_to(names[b, 0:1, :], (128, count)).T
        tall[...] = jnp.full(tall.shape, -1.0, jnp.float32)

    def pair(a, b):
        left = near[...]
        best = tall[...]
        scores = lax.dot_general(rows[b], rows[a], NT, preferred_element_type=jnp.float32)
        for low in range(0, count, 128):
            tile = scores[:, low:low + 128]
            match = left == names[a, 0:1, low:low + 128]
            if a == b:
                i = lax.broadcasted_iota(jnp.int32, tile.shape, 0)
                j = lax.broadcasted_iota(jnp.int32, tile.shape, 1) + low
                match = match & (i != j)
            tile = jnp.where(match, tile, jnp.float32(-1.0))
            best = jnp.maximum(best, tile)
            if a != b:
                up = jnp.max(tile.reshape(count // 8, 8, 128), axis=0)
                held[a, :, low:low + 128] = jnp.maximum(held[a, :, low:low + 128], up)
        tall[...] = best

    def close_step(b):
        held[b] = jnp.max(tall[...].T.reshape(128 // 8, 8, count), axis=0)

    def program(who):
        for chunk in range(CHUNKS):
            forward(who, 0, chunk)
        for kind, one, two in TASKS[who]:
            if kind == 0:
                chunk_copy(0, one, two, twin).wait_recv()
                if two == 0:
                    name_copy(0, one, twin).wait_recv()
                forward(who, one, two)
            elif kind == 1:
                pair_copy(one, two).start()
                pair_name_copy(one, two).start()
            elif kind == 2:
                if one >= SLOTS:
                    pair_copy(0, one - SLOTS).wait_recv()
                    pair_name_copy(0, one - SLOTS).wait_recv()
                open_step(one)
            elif kind == 3:
                pair(one, two)
            elif kind == 4:
                close_step(one)
            else:
                leaving[one] = jnp.max(held[one], axis=0, keepdims=True)
                result_copy(who, one).start()

        given, taken = len(SHARED[who]), len(SHARED[1 - who])
        own, other = results.at[1:SLOTS], results.at[SLOTS:SLOTS + given]
        remote(own, own, result_send, result_recv.at[0], twin).wait_recv()
        remote(other, other, result_send, result_recv.at[1], twin).wait_recv()
        top = jnp.max(held[0], axis=0, keepdims=True)
        for node in range(1, SLOTS + given):
            top = jnp.maximum(top, results[node])
        out_ref[...] = top

        def drain(ref, sem):
            remote(ref, ref, sem, sem, twin).wait_send()

        drain(rows.at[1:SLOTS], row_send)
        drain(names.at[1:SLOTS], name_send)
        drain(rows.at[0:given], pair_send)
        drain(names.at[0:given], pname_send)
        drain(results.at[1:SLOTS + taken], result_send)

    for who in range(2):
        pl.when(core == who)(lambda who=who: program(who))


def on_device(embeddings, cluster):
    count, width = embeddings.shape
    dma = pltpu.SemaphoreType.DMA
    best = pl.pallas_call(
        kernel,
        out_shape=jax.ShapeDtypeStruct((1, count), jnp.float32),
        in_specs=[pl.BlockSpec(memory_space=pl.ANY)] * 2,
        out_specs=pl.BlockSpec(memory_space=pltpu.VMEM),
        scratch_shapes=[
            pltpu.VMEM((count, width), jnp.bfloat16),
            pltpu.VMEM((1, count), jnp.int32),
            pltpu.VMEM((NODES, count, width), jnp.bfloat16),
            pltpu.VMEM((NODES, 8, count), jnp.float32),
            pltpu.VMEM((NODES, 8, count), jnp.float32),
            pltpu.VMEM((NODES, 1, count), jnp.float32),
            pltpu.VMEM((NODES, 1, count), jnp.float32),
            pltpu.VMEM((count, 128), jnp.float32),
            pltpu.VMEM((count, 128), jnp.float32),
            dma((2,)), dma(()), dma((SLOTS, CHUNKS)), dma(()), dma((SLOTS,)),
            dma(()), dma((TAKEN,)), dma(()), dma((TAKEN,)),
            dma(()), dma((2,)),
        ],
        compiler_params=pltpu.CompilerParams(
            collective_id=0, has_side_effects=True, vmem_limit_bytes=56 * 2**20),
    )(embeddings, cluster.reshape(1, count))
    return best.reshape(count)


def solution(mesh):
    return jax.shard_map(
        on_device,
        mesh=mesh,
        in_specs=(P(("owner", "rep"), None), P(("owner", "rep"))),
        out_specs=P(("owner", "rep")),
        check_vma=False,
    )
```

time: 47 us -> 45.2 us (0.962)
  Pallas kernels: 45.7 us -> 43.8 us
    pallas_call x1, Pallas kernels: 45.7 us -> 43.8 us  [on_device(): pl.pallas_call(kernel, out_shape=jax.ShapeDtypeStruct((1, count), jnp.flo...]
where the time goes in v3:
time: 45.2 us; the launch traced here: 45 us
  Pallas kernels  43.8 us (97%)
  local copies, waits for them, and re-layouts  1.22 us (3%)
    pallas_call x1, Pallas kernels, on_device(): pl.pallas_call(kernel, out_shape=jax.ShapeDtypeStruct((1, count), jnp.flo...  43.8 us
    unnamed x3, local copies, waits for them, and re-layouts  1.22 us

profile of v3, /device:TPU:1, one launch (start us, length us, event | category | flops | bytes accessed | tf_op | source)
XLA Modules:
  0.0 45.0 jit_solution(4758845109150480415)
XLA Ops:
  0.0 43.8 %shard_map.28 = f32[1,256]{1,0:T(1,128)} custom-call(bf16[256,1024]{1,0:T(8,128)(2,1)} %emb_ref.1, s32[1,256]{1,0:T(1,128)} %bitcast.3), custom_call_target="tpu_custom_call" | custom-call | tf_op jit(solution)/shard_map/pallas_call | solution.py:266
  43.8 0.0 copy-start
  43.8 0.7 %copy-done = f32[1,256]{1,0:T(1,128)S(1)} copy-done((f32[1,256]{1,0:T(1,128)S(1)}, f32[1,256]{1,0:T(1,128)}, u32[]{:S(2)}) %copy-start) | copy-done | bytes 1048
  44.4 0.6 %copy.4 = f32[256]{0:T(256)} copy(f32[256]{0:T(256)S(1)} %bitcast.2) | data formatting | bytes 2048
Async XLA Ops:
  43.8 0.7 %copy-start = (f32[1,256]{1,0:T(1,128)S(1)}, f32[1,256]{1,0:T(1,128)}, u32[]{:S(2)}) copy-start(f32[1,256]{1,0:T(1,128)} %shard_map.28) | copy-start | bytes 3076

commit v4 on v3

v4 whole, which is shorter than its diff:
```python
import jax
import jax.numpy as jnp
from jax import lax
from jax.experimental import pallas as pl
from jax.experimental.pallas import tpu as pltpu
from jax.sharding import PartitionSpec as P

MESH = pl.DeviceIdType.MESH
SIDE = 4
HOME = (0, 0, 0)
STEPS = ((1, 0, 0), (-1, 0, 0), (0, 1, 0), (0, -1, 0), (0, 0, 1), (0, 0, -1))
SPOTS = (
    ((0, 0, 0), (1, 0, 0), (0, 1, 0), (0, 0, 1), (1, 3, 0), (2, 0, 0), (0, 1, 3), (0, 0, 2), (0, 2, 0), (3, 1, 3), (2, 3, 0), (3, 1, 2)),
    ((0, 0, 0), (3, 0, 0), (0, 0, 3), (0, 3, 0), (2, 0, 0), (0, 1, 3), (0, 3, 1), (0, 0, 2), (2, 3, 0), (1, 1, 3), (3, 0, 2), (2, 2, 0)),
)
SHARED = ((0, 1, 2, 3, 4, 5, 6, 7, 8, 9), (0, 1, 2, 3, 4, 5, 6, 7, 8))
PARENT = (
    (
        (-1, 0, 0, 0, 1, 1, 2, 3, 2, 6, 4, 9),
        (-1, 0, 0, 0, 1, 1, 2, 3, 2, 6, 4, 9),
        (-1, 0, 0, 0, 1, 1, 2, 3, 2, 6, 4, 9),
        (-1, 0, 0, 0, 1, 1, 2, 3, 2, 6, 4, 9),
    ),
    (
        (-1, 0, 0, 0, 1, 2, 3, 2, 4, 5, 7, 8),
        (-1, 0, 0, 0, 1, 2, 3, 2, 4, 5, 7, 8),
        (-1, 0, 0, 0, 1, 2, 3, 2, 4, 5, 7, 8),
        (-1, 0, 0, 0, 1, 2, 3, 2, 4, 5, 7, 8),
    ),
)
WAY = (
    (
        (-1, 0, 2, 4, 3, 0, 5, 4, 2, 1, 0, 5),
        (-1, 0, 2, 4, 3, 0, 5, 4, 2, 1, 0, 5),
        (-1, 0, 2, 4, 3, 0, 5, 4, 2, 1, 0, 5),
        (-1, 0, 2, 4, 3, 0, 5, 4, 2, 1, 0, 5),
    ),
    (
        (-1, 1, 5, 3, 1, 2, 4, 5, 3, 0, 1, 3),
        (-1, 1, 5, 3, 1, 2, 4, 5, 3, 0, 1, 3),
        (-1, 1, 5, 3, 1, 2, 4, 5, 3, 0, 1, 3),
        (-1, 1, 5, 3, 1, 2, 4, 5, 3, 0, 1, 3),
    ),
)
ORDER = (
    (
        (2, 1, 6, 3, 4, 9, 5, 7, 8, 10, 11),
        (2, 1, 6, 3, 4, 9, 5, 7, 8, 10, 11),
        (2, 1, 6, 3, 4, 9, 5, 7, 8, 10, 11),
        (2, 1, 6, 3, 4, 9, 5, 7, 8, 10, 11),
    ),
    (
        (1, 2, 4, 3, 5, 7, 8, 6, 9, 10, 11),
        (1, 2, 4, 3, 5, 7, 8, 6, 9, 10, 11),
        (1, 2, 4, 3, 5, 7, 8, 6, 9, 10, 11),
        (1, 2, 4, 3, 5, 7, 8, 6, 9, 10, 11),
    ),
)
TASKS = (
    (
        (1, 0, 0), (2, 0, 0), (3, 0, 0), (4, 0, 0), (0, 1, 0), (0, 2, 0), (0, 3, 0), (2, 12, 0), (3, 0, 12),
        (4, 12, 0), (0, 1, 1), (0, 2, 1), (0, 3, 1), (0, 1, 2), (0, 2, 2), (0, 3, 2), (0, 1, 3), (1, 1, 1),
        (2, 1, 0), (3, 0, 1), (4, 1, 0), (0, 4, 0), (0, 6, 0), (0, 2, 3), (0, 3, 3), (1, 2, 2), (1, 3, 3),
        (2, 2, 0), (3, 12, 2), (3, 0, 2), (3, 1, 2), (4, 2, 0), (2, 3, 0), (3, 0, 3), (3, 1, 3), (3, 2, 3),
        (4, 3, 0), (0, 4, 1), (2, 13, 0), (3, 1, 13), (4, 13, 0), (0, 6, 1), (2, 14, 0), (4, 14, 0),
        (0, 4, 2), (2, 15, 0), (3, 2, 15), (4, 15, 0), (0, 6, 2), (0, 4, 3), (0, 9, 0), (1, 4, 4), (2, 4, 0),
        (3, 2, 4), (3, 12, 4), (3, 14, 4), (3, 3, 4), (3, 13, 4), (4, 4, 0), (0, 5, 0), (0, 5, 1), (0, 5, 2),
        (0, 5, 3), (1, 5, 5), (2, 5, 0), (3, 2, 5), (3, 0, 5), (3, 14, 5), (3, 3, 5), (3, 15, 5), (3, 13, 5),
        (3, 4, 5), (4, 5, 0), (0, 6, 3), (0, 9, 1), (1, 6, 6), (2, 6, 0), (3, 1, 6), (3, 3, 6), (3, 13, 6),
        (3, 4, 6), (3, 5, 6), (4, 6, 0), (2, 16, 0), (4, 16, 0), (0, 7, 0), (0, 7, 1), (0, 7, 2), (0, 7, 3),
        (1, 7, 7), (0, 8, 0), (0, 8, 1), (0, 8, 2), (0, 8, 3), (1, 8, 8), (2, 7, 0), (3, 1, 7), (3, 0, 7),
        (3, 6, 7), (3, 14, 7), (3, 13, 7), (3, 16, 7), (3, 4, 7), (3, 15, 7), (3, 5, 7), (4, 7, 0), (5, 1, 0),
        (0, 9, 2), (2, 8, 0), (3, 0, 8), (3, 14, 8), (3, 13, 8), (3, 16, 8), (3, 3, 8), (3, 15, 8), (3, 5, 8),
        (3, 7, 8), (4, 8, 0), (5, 16, 0), (5, 13, 0), (5, 14, 0), (0, 9, 3), (2, 17, 0), (3, 7, 17),
        (4, 17, 0), (1, 9, 9), (2, 18, 0), (3, 6, 18), (4, 18, 0), (5, 6, 0), (2, 19, 0), (4, 19, 0),
        (2, 9, 0), (3, 2, 9), (3, 8, 9), (3, 15, 9), (3, 4, 9), (3, 5, 9), (3, 19, 9), (3, 12, 9), (3, 18, 9),
        (4, 9, 0), (5, 8, 0), (5, 2, 0), (5, 15, 0), (2, 20, 0), (3, 9, 20), (4, 20, 0), (5, 20, 0),
        (0, 10, 0), (0, 10, 1), (0, 10, 2), (0, 10, 3), (2, 10, 0), (3, 7, 10), (3, 3, 10), (3, 9, 10),
        (3, 19, 10), (3, 18, 10), (3, 17, 10), (4, 10, 0), (5, 9, 0), (5, 7, 0), (5, 19, 0), (5, 3, 0),
        (0, 11, 0), (0, 11, 1), (0, 11, 2), (0, 11, 3), (2, 11, 0), (3, 4, 11), (3, 5, 11), (3, 10, 11),
        (3, 17, 11), (3, 12, 11), (3, 18, 11), (4, 11, 0), (5, 11, 0), (5, 10, 0), (5, 4, 0), (5, 5, 0),
        (5, 17, 0), (5, 18, 0), (5, 12, 0),
    ),
    (
        (1, 0, 0), (2, 0, 0), (3, 0, 0), (4, 0, 0), (0, 1, 0), (0, 2, 0), (0, 3, 0), (2, 12, 0), (4, 12, 0),
        (0, 1, 1), (0, 2, 1), (0, 3, 1), (0, 1, 2), (0, 2, 2), (0, 3, 2), (0, 1, 3), (1, 1, 1), (2, 1, 0),
        (3, 12, 1), (3, 0, 1), (4, 1, 0), (0, 5, 0), (0, 2, 3), (0, 3, 3), (0, 4, 0), (1, 2, 2), (1, 3, 3),
        (2, 2, 0), (3, 12, 2), (3, 0, 2), (3, 1, 2), (4, 2, 0), (2, 3, 0), (3, 0, 3), (3, 1, 3), (3, 2, 3),
        (4, 3, 0), (0, 4, 1), (2, 13, 0), (3, 3, 13), (3, 2, 13), (4, 13, 0), (0, 5, 1), (0, 7, 0),
        (2, 14, 0), (3, 2, 14), (4, 14, 0), (2, 15, 0), (3, 2, 15), (4, 15, 0), (0, 4, 2), (0, 5, 2),
        (0, 7, 1), (0, 8, 0), (0, 4, 3), (1, 4, 4), (2, 4, 0), (3, 0, 4), (3, 2, 4), (3, 3, 4), (4, 4, 0),
        (0, 8, 1), (0, 5, 3), (0, 7, 2), (2, 16, 0), (3, 4, 16), (4, 16, 0), (1, 5, 5), (0, 6, 0), (0, 6, 1),
        (0, 6, 2), (0, 6, 3), (1, 6, 6), (2, 5, 0), (3, 4, 5), (3, 3, 5), (3, 12, 5), (3, 15, 5), (3, 16, 5),
        (3, 1, 5), (4, 5, 0), (0, 8, 2), (0, 7, 3), (2, 6, 0), (3, 2, 6), (3, 12, 6), (3, 16, 6), (3, 14, 6),
        (3, 1, 6), (3, 5, 6), (4, 6, 0), (1, 7, 7), (2, 17, 0), (3, 6, 17), (3, 5, 17), (4, 17, 0), (0, 8, 3),
        (2, 18, 0), (4, 18, 0), (1, 8, 8), (2, 7, 0), (3, 16, 7), (3, 0, 7), (3, 4, 7), (3, 5, 7), (3, 1, 7),
        (4, 7, 0), (5, 16, 0), (2, 19, 0), (4, 19, 0), (2, 20, 0), (4, 20, 0), (2, 8, 0), (3, 5, 8),
        (3, 1, 8), (3, 15, 8), (3, 13, 8), (3, 7, 8), (3, 19, 8), (3, 18, 8), (4, 8, 0), (5, 5, 0), (0, 9, 0),
        (0, 9, 1), (0, 9, 2), (0, 9, 3), (2, 9, 0), (3, 12, 9), (3, 15, 9), (3, 3, 9), (3, 7, 9), (3, 6, 9),
        (3, 8, 9), (3, 14, 9), (3, 19, 9), (4, 9, 0), (5, 15, 0), (5, 12, 0), (2, 21, 0), (4, 21, 0),
        (0, 10, 0), (0, 10, 1), (0, 10, 2), (0, 10, 3), (2, 10, 0), (3, 2, 10), (3, 3, 10), (3, 9, 10),
        (3, 6, 10), (3, 8, 10), (3, 14, 10), (3, 20, 10), (3, 17, 10), (3, 18, 10), (4, 10, 0), (5, 8, 0),
        (5, 9, 0), (5, 10, 0), (5, 6, 0), (5, 17, 0), (5, 20, 0), (5, 2, 0), (5, 3, 0), (5, 14, 0),
        (0, 11, 0), (0, 11, 1), (0, 11, 2), (0, 11, 3), (2, 11, 0), (3, 0, 11), (3, 1, 11), (3, 4, 11),
        (3, 7, 11), (3, 21, 11), (3, 19, 11), (3, 18, 11), (3, 13, 11), (4, 11, 0), (5, 11, 0), (5, 21, 0),
        (5, 4, 0), (5, 7, 0), (5, 18, 0), (5, 19, 0), (5, 1, 0), (5, 13, 0),
    ),
)
SLOTS = len(SPOTS[0])
TAKEN = max(len(shared) for shared in SHARED)
NODES = SLOTS + TAKEN
CHUNKS = len(PARENT[0])
NT = (((1,), (1,)), ((), ()))


def place():
    owner, z = lax.axis_index("owner"), lax.axis_index("rep")
    return owner // (2 * SIDE), (owner // 2) % SIDE, owner % 2, z


def kernel(
    emb_ref, cluster_ref, out_ref, raw, label, rows, names, held, leaving, results,
    load_sem, row_send, row_recv, name_send, name_recv, pair_send, pair_recv,
    pname_send, pname_recv, result_send, result_recv,
):
    x, y, core, z = place()
    count = raw.shape[0]
    part = count // CHUNKS

    def wrap(v):
        return jnp.where(v >= SIDE, v - SIDE, v)

    def at(step, flip):
        nx, ny, nz = (wrap(v + d % SIDE) for v, d in zip((x, y, z), step))
        return (nx * SIDE + ny) * 2 + (1 - core if flip else core), nz

    loads = (
        pltpu.make_async_copy(emb_ref, raw, load_sem.at[0]),
        pltpu.make_async_copy(cluster_ref, label, load_sem.at[1]),
    )
    for load in loads:
        load.start()
    barrier = pltpu.get_barrier_semaphore()
    near_by = [at(step, 0) for step in STEPS]
    twin = at(HOME, 1)
    for spot in near_by + [twin]:
        pl.semaphore_signal(barrier, 1, device_id=spot, device_id_type=MESH)
    homes = [[
        at(tuple(-v for v in SPOTS[who][node]), 0) if node < SLOTS else
        at(tuple(-v for v in SPOTS[1 - who][SHARED[1 - who][node - SLOTS]]), 1)
        for node in range(SLOTS + len(SHARED[1 - who]))] for who in range(2)]
    for load in loads:
        load.wait()

    values = raw[...].astype(jnp.float32)
    factor = lax.rsqrt(jnp.mean(values * values, axis=1, keepdims=True) + 1e-06)
    rows[0] = (values * (factor * raw.shape[1] ** (-0.5))).astype(jnp.bfloat16)
    names[0] = jnp.broadcast_to(label[...].astype(jnp.float32), names.shape[1:])
    pl.semaphore_wait(barrier, len(STEPS) + 1)

    def remote(src, dst, send, recv, spot):
        return pltpu.make_async_remote_copy(
            src, dst, send, recv, device_id=spot, device_id_type=MESH)

    def chunk_copy(src, dst, chunk, spot):
        span = pl.ds(chunk * part, part)
        return remote(rows.at[src, span], rows.at[dst, span], row_send, row_recv.at[dst, chunk], spot)

    def name_copy(src, dst, spot):
        return remote(names.at[src], names.at[dst], name_send, name_recv.at[dst], spot)

    def pair_copy(slot, i):
        return remote(rows.at[slot], rows.at[SLOTS + i], pair_send, pair_recv.at[i], twin)

    def pair_name_copy(slot, i):
        return remote(names.at[slot], names.at[SLOTS + i], pname_send, pname_recv.at[i], twin)

    def result_copy(who, node):
        flip = int(node >= SLOTS)
        return remote(leaving.at[node], results.at[node], result_send, result_recv.at[flip],
                      homes[who][node])

    def forward(who, slot, chunk):
        for k in ORDER[who][chunk]:
            if PARENT[who][chunk][k] == slot:
                spot = near_by[WAY[who][chunk][k]]
                chunk_copy(slot, k, chunk, spot).start()
                if chunk == 0:
                    name_copy(slot, k, spot).start()

    def open_step(b):
        return jnp.broadcast_to(names[b, 0:1, :], (128, count)).T

    def pair(a, b, left, best):
        scores = lax.dot_general(rows[b], rows[a], NT, preferred_element_type=jnp.float32)
        for low in range(0, count, 128):
            tile = scores[:, low:low + 128]
            match = left == names[a, 0:1, low:low + 128]
            if a == b:
                i = lax.broadcasted_iota(jnp.int32, tile.shape, 0)
                j = lax.broadcasted_iota(jnp.int32, tile.shape, 1) + low
                match = match & (i != j)
            tile = jnp.where(match, tile, jnp.float32(-1.0))
            best = jnp.maximum(best, tile)
            if a != b:
                up = jnp.max(tile.reshape(count // 8, 8, 128), axis=0)
                held[a, :, low:low + 128] = jnp.maximum(held[a, :, low:low + 128], up)
        return best

    def close_step(b, best):
        held[b] = jnp.max(best.T.reshape(128 // 8, 8, count), axis=0)

    def program(who):
        for chunk in range(CHUNKS):
            forward(who, 0, chunk)
        for kind, one, two in TASKS[who]:
            if kind == 0:
                chunk_copy(0, one, two, twin).wait_recv()
                if two == 0:
                    name_copy(0, one, twin).wait_recv()
                forward(who, one, two)
            elif kind == 1:
                pair_copy(one, two).start()
                pair_name_copy(one, two).start()
            elif kind == 2:
                if one >= SLOTS:
                    pair_copy(0, one - SLOTS).wait_recv()
                    pair_name_copy(0, one - SLOTS).wait_recv()
                left = open_step(one)
                best = jnp.full(left.shape, -1.0, jnp.float32)
            elif kind == 3:
                best = pair(one, two, left, best)
            elif kind == 4:
                close_step(one, best)
            else:
                leaving[one] = jnp.max(held[one], axis=0, keepdims=True)
                result_copy(who, one).start()

        given, taken = len(SHARED[who]), len(SHARED[1 - who])
        own, other = results.at[1:SLOTS], results.at[SLOTS:SLOTS + given]
        remote(own, own, result_send, result_recv.at[0], twin).wait_recv()
        remote(other, other, result_send, result_recv.at[1], twin).wait_recv()
        top = jnp.max(held[0], axis=0, keepdims=True)
        for node in range(1, SLOTS + given):
            top = jnp.maximum(top, results[node])
        out_ref[...] = top

        def drain(ref, sem):
            remote(ref, ref, sem, sem, twin).wait_send()

        drain(rows.at[1:SLOTS], row_send)
        drain(names.at[1:SLOTS], name_send)
        drain(rows.at[0:given], pair_send)
        drain(names.at[0:given], pname_send)
        drain(results.at[1:SLOTS + taken], result_send)

    for who in range(2):
        pl.when(core == who)(lambda who=who: program(who))


def on_device(embeddings, cluster):
    count, width = embeddings.shape
    dma = pltpu.SemaphoreType.DMA
    best = pl.pallas_call(
        kernel,
        out_shape=jax.ShapeDtypeStruct((1, count), jnp.float32),
        in_specs=[pl.BlockSpec(memory_space=pl.ANY)] * 2,
        out_specs=pl.BlockSpec(memory_space=pltpu.VMEM),
        scratch_shapes=[
            pltpu.VMEM((count, width), jnp.bfloat16),
            pltpu.VMEM((1, count), jnp.int32),
            pltpu.VMEM((NODES, count, width), jnp.bfloat16),
            pltpu.VMEM((NODES, 8, count), jnp.float32),
            pltpu.VMEM((NODES, 8, count), jnp.float32),
            pltpu.VMEM((NODES, 1, count), jnp.float32),
            pltpu.VMEM((NODES, 1, count), jnp.float32),
            dma((2,)), dma(()), dma((SLOTS, CHUNKS)), dma(()), dma((SLOTS,)),
            dma(()), dma((TAKEN,)), dma(()), dma((TAKEN,)),
            dma(()), dma((2,)),
        ],
        compiler_params=pltpu.CompilerParams(
            collective_id=0, has_side_effects=True, vmem_limit_bytes=56 * 2**20),
    )(embeddings, cluster.reshape(1, count))
    return best.reshape(count)


def solution(mesh):
    return jax.shard_map(
        on_device,
        mesh=mesh,
        in_specs=(P(("owner", "rep"), None), P(("owner", "rep"))),
        out_specs=P(("owner", "rep")),
        check_vma=False,
    )
```

time: 45.2 us -> 44.1 us (0.976)
  Pallas kernels: 43.8 us -> 42.7 us
    pallas_call x1, Pallas kernels: 43.8 us -> 42.7 us  [on_device(): pl.pallas_call(kernel, out_shape=jax.ShapeDtypeStruct((1, count), jnp.flo...]
where the time goes in v4:
time: 44.1 us; the launch traced here: 43.9 us
  Pallas kernels  42.7 us (97%)
  local copies, waits for them, and re-layouts  1.22 us (3%)
    pallas_call x1, Pallas kernels, on_device(): pl.pallas_call(kernel, out_shape=jax.ShapeDtypeStruct((1, count), jnp.flo...  42.7 us
    unnamed x3, local copies, waits for them, and re-layouts  1.22 us

profile of v4, /device:TPU:1, one launch (start us, length us, event | category | flops | bytes accessed | tf_op | source)
XLA Modules:
  0.0 43.9 jit_solution(14718761935534841778)
XLA Ops:
  0.0 42.7 %shard_map.28 = f32[1,256]{1,0:T(1,128)} custom-call(bf16[256,1024]{1,0:T(8,128)(2,1)} %emb_ref.1, s32[1,256]{1,0:T(1,128)} %bitcast.3), custom_call_target="tpu_custom_call" | custom-call | tf_op jit(solution)/shard_map/pallas_call | solution.py:264
  42.7 0.0 copy-start
  42.7 0.7 %copy-done = f32[1,256]{1,0:T(1,128)S(1)} copy-done((f32[1,256]{1,0:T(1,128)S(1)}, f32[1,256]{1,0:T(1,128)}, u32[]{:S(2)}) %copy-start) | copy-done | bytes 1048
  43.4 0.6 %copy.4 = f32[256]{0:T(256)} copy(f32[256]{0:T(256)S(1)} %bitcast.2) | data formatting | bytes 2048
Async XLA Ops:
  42.7 0.7 %copy-start = (f32[1,256]{1,0:T(1,128)S(1)}, f32[1,256]{1,0:T(1,128)}, u32[]{:S(2)}) copy-start(f32[1,256]{1,0:T(1,128)} %shard_map.28) | copy-start | bytes 3076

commit v5 on v4

--- a/solution.py
+++ b/solution.py
@@ -155,7 +155,7 @@
     values = raw[...].astype(jnp.float32)
     factor = lax.rsqrt(jnp.mean(values * values, axis=1, keepdims=True) + 1e-06)
     rows[0] = (values * (factor * raw.shape[1] ** (-0.5))).astype(jnp.bfloat16)
-    names[0] = jnp.broadcast_to(label[...].astype(jnp.float32), names.shape[1:])
+    names[0] = label[...].astype(jnp.float32)
     pl.semaphore_wait(barrier, len(STEPS) + 1)
 
     def remote(src, dst, send, recv, spot):
@@ -270,7 +270,7 @@
             pltpu.VMEM((count, width), jnp.bfloat16),
             pltpu.VMEM((1, count), jnp.int32),
             pltpu.VMEM((NODES, count, width), jnp.bfloat16),
-            pltpu.VMEM((NODES, 8, count), jnp.float32),
+            pltpu.VMEM((NODES, 1, count), jnp.float32),
             pltpu.VMEM((NODES, 8, count), jnp.float32),
             pltpu.VMEM((NODES, 1, count), jnp.float32),
             pltpu.VMEM((NODES, 1, count), jnp.float32),

time: 44.1 us -> 44 us (level)
  no operation moved by 1% of the time
where the time goes in v5:
time: 44 us; the launch traced here: 43.6 us
  Pallas kernels  42.3 us (96%)
  local copies, waits for them, and re-layouts  1.22 us (3%)
    pallas_call x1, Pallas kernels, on_device(): pl.pallas_call(kernel, out_shape=jax.ShapeDtypeStruct((1, count), jnp.flo...  42.3 us
    unnamed x3, local copies, waits for them, and re-layouts  1.22 us

profile of v5, /device:TPU:1, one launch (start us, length us, event | category | flops | bytes accessed | tf_op | source)
XLA Modules:
  0.0 43.6 jit_solution(3064509102537906273)
XLA Ops:
  0.0 42.3 %shard_map.28 = f32[1,256]{1,0:T(1,128)} custom-call(bf16[256,1024]{1,0:T(8,128)(2,1)} %emb_ref.1, s32[1,256]{1,0:T(1,128)} %bitcast.3), custom_call_target="tpu_custom_call" | custom-call | tf_op jit(solution)/shard_map/pallas_call | solution.py:264
  42.4 0.0 copy-start
  42.4 0.7 %copy-done = f32[1,256]{1,0:T(1,128)S(1)} copy-done((f32[1,256]{1,0:T(1,128)S(1)}, f32[1,256]{1,0:T(1,128)}, u32[]{:S(2)}) %copy-start) | copy-done | bytes 1048
  43.0 0.6 %copy.4 = f32[256]{0:T(256)} copy(f32[256]{0:T(256)S(1)} %bitcast.2) | data formatting | bytes 2048
Async XLA Ops:
  42.4 0.7 %copy-start = (f32[1,256]{1,0:T(1,128)S(1)}, f32[1,256]{1,0:T(1,128)}, u32[]{:S(2)}) copy-start(f32[1,256]{1,0:T(1,128)} %shard_map.28) | copy-start | bytes 3076
